TPU v7x, 32 devices: a whole 2x2x4 slice. The times are simulated.
32 devices in a mesh: sh: 4 (over z), sw: 4 (over y, core), tp: 2 (over x).
Axes of the slice: x: 2, y: 2, z: 4, core: 2. Of those that a mesh axis runs over, the one named last changes fastest.
Arguments:
- queries: bfloat16 [2, 32, 32, 1536], P('tp', 'sh', 'sw'), may hold values from -6 to 6
- keys: bfloat16 [2, 32, 32, 1536], P('tp', 'sh', 'sw'), may hold values from -6 to 6
- values: bfloat16 [2, 32, 32, 1536], P('tp', 'sh', 'sw'), may hold values from -6 to 6
- attn_out: bfloat16 [2, 32, 32, 1536], P('tp', 'sh', 'sw'), may hold values from -6 to 6
- attn_grad: bfloat16 [2, 32, 32, 1536], P('tp', 'sh', 'sw'), may hold values from -192 to 192
- log_sum: float32 [2, 32, 32, 12], P('tp', 'sh', 'sw'), may hold values from 6.1 to 6.9
- window_dirs: int32 [12, 4], replicated, may hold values from 0 to 7, as said below
Outputs:
- q_grad: bfloat16 [2, 32, 32, 1536], P('tp', 'sh', 'sw')
- k_grad: bfloat16 [2, 32, 32, 1536], P('tp', 'sh', 'sw')
- v_grad: bfloat16 [2, 32, 32, 1536], P('tp', 'sh', 'sw')
Inputs may be any that keep to these rules, and one draw needn't show every extreme that they name: `window_dirs`: each row names 4 different directions. Within each run of 6 consecutive heads (those of one index of tp) every direction is named by exactly half of the rows.
All inputs are finite; a program needn't handle non-finite values.
Results may differ from a plain program's by a relative error of at most 0.0056.
Values may be sent and summed in bfloat16 or wider, within the bound.
A program may use at most 64 MiB of HBM per device.

v0:
```python
import jax
import jax.numpy as jnp
from jax import lax
from jax.sharding import PartitionSpec as P

NEIGHBOURS = ((-1, -1), (-1, 0), (-1, 1), (0, -1), (0, 1), (1, -1), (1, 0), (1, 1))


def passed_along(block, axis, distance):
    devices = range(lax.axis_size(axis))
    route = [(i - distance, i) for i in devices if i - distance in devices]
    return lax.ppermute(block, axis, route)


def slot_tables(local_dirs):
    head_count = local_dirs.shape[0]
    half_heads = head_count // 2
    directions = jnp.arange(8, dtype=jnp.int32)
    listed = (local_dirs[:, :, None] == directions[None, None, :]).astype(jnp.int32)
    member = jnp.sum(listed, axis=1)
    position = jnp.sum(listed * jnp.arange(4, dtype=jnp.int32)[None, :, None], axis=1)
    rank_in = jnp.cumsum(member, axis=0) - 1
    slot_of = jnp.sum(listed * rank_in[:, None, :], axis=2)
    chosen = member[:, :, None] * (
        rank_in[:, :, None] == jnp.arange(half_heads, dtype=jnp.int32)[None, None, :]
    ).astype(jnp.int32)
    head_ids = jnp.arange(head_count, dtype=jnp.int32)
    head_of = jnp.sum(chosen * head_ids[:, None, None], axis=0)
    place_of = jnp.sum(chosen * position[:, :, None], axis=0)
    return (slot_of, head_of, place_of)


def bounds(offsets, direction_sign):
    grid_row = lax.axis_index("sh")
    grid_col = lax.axis_index("sw")
    target_row = grid_row + direction_sign * offsets[:, 0]
    target_col = grid_col + direction_sign * offsets[:, 1]
    inside = (
        (target_row >= 0)
        & (target_row < lax.axis_size("sh"))
        & (target_col >= 0)
        & (target_col < lax.axis_size("sw"))
    )
    return inside.astype(jnp.float32)


def pull_blocks(packs):
    arrived = {}
    for step_row in (-1, 1):
        stacked = jnp.stack(
            [packs[NEIGHBOURS.index((step_row, step_col))] for step_col in (-1, 0, 1)]
        )
        arrived[step_row] = passed_along(stacked, "sh", -step_row)
    result = {}
    for step_row in (-1, 1):
        result[step_row, 0] = arrived[step_row][1]
    for step_col in (-1, 1):
        column_pick = 0 if step_col < 0 else 2
        stacked = jnp.stack(
            [
                arrived[-1][column_pick],
                packs[NEIGHBOURS.index((0, step_col))],
                arrived[1][column_pick],
            ]
        )
        shifted = passed_along(stacked, "sw", -step_col)
        result[-1, step_col] = shifted[0]
        result[0, step_col] = shifted[1]
        result[1, step_col] = shifted[2]
    return jnp.stack([result[offset_pair] for offset_pair in NEIGHBOURS])


def send_out(packs, along_cols, along_rows):
    arrived = {}
    for step_col in (-1, 1):
        stacked = jnp.stack(
            [packs[NEIGHBOURS.index((step_row, step_col))] for step_row in (-1, 0, 1)]
        )
        arrived[step_col] = along_cols(stacked, step_col)
    result = {}
    for step_col in (-1, 1):
        result[0, step_col] = arrived[step_col][1]
    for step_row in (-1, 1):
        row_pick = 0 if step_row < 0 else 2
        stacked = jnp.stack(
            [arrived[-1][row_pick], packs[NEIGHBOURS.index((step_row, 0))], arrived[1][row_pick]]
        )
        shifted = along_rows(stacked, step_row)
        result[step_row, -1] = shifted[0]
        result[step_row, 0] = shifted[1]
        result[step_row, 1] = shifted[2]
    return jnp.stack([result[offset_pair] for offset_pair in NEIGHBOURS])


def local(queries, keys, values, attn_out, attn_grad, log_sum, window_dirs):
    frames_here, tile_rows, tile_cols, width_all = queries.shape
    head_total = log_sum.shape[3]
    head_dim = width_all // head_total
    row_delta = jnp.sum(
        (attn_grad.astype(jnp.float32) * attn_out.astype(jnp.float32)).reshape(
            frames_here, tile_rows, tile_cols, head_total, head_dim
        ),
        axis=4,
    )
    q_heads, k_heads, v_heads, g_heads = (
        lax.all_to_all(queries, "tp", split_axis=3, concat_axis=0, tiled=True),
        lax.all_to_all(keys, "tp", split_axis=3, concat_axis=0, tiled=True),
        lax.all_to_all(values, "tp", split_axis=3, concat_axis=0, tiled=True),
        lax.all_to_all(attn_grad, "tp", split_axis=3, concat_axis=0, tiled=True),
    )
    lse_heads, delta_heads = (
        lax.all_to_all(log_sum, "tp", split_axis=3, concat_axis=0, tiled=True),
        lax.all_to_all(row_delta, "tp", split_axis=3, concat_axis=0, tiled=True),
    )
    frames_all = q_heads.shape[0]
    head_here = q_heads.shape[3] // head_dim
    tile_tok = frames_all * tile_rows * tile_cols
    score_scale = head_dim ** (-0.5)

    def by_head(array):
        return jnp.transpose(array.reshape(tile_tok, head_here, head_dim), (1, 0, 2))

    q_own = by_head(q_heads)
    k_own = by_head(k_heads)
    v_own = by_head(v_heads)
    g_own = by_head(g_heads)
    lse_own = lse_heads.reshape(tile_tok, head_here).T
    delta_own = delta_heads.reshape(tile_tok, head_here).T
    local_dirs = lax.dynamic_slice_in_dim(
        window_dirs, lax.axis_index("tp") * head_here, head_here, 0
    )
    slot_of, head_of, place_of = slot_tables(local_dirs)
    offsets = jnp.array(NEIGHBOURS, dtype=jnp.int32)
    ahead_live = bounds(offsets, 1)
    kv_own = jnp.stack([k_own, v_own], axis=1)
    kv_packs = [jnp.take(kv_own, head_of[direction], axis=0) for direction in range(8)]
    recv_kv = pull_blocks(kv_packs)
    nb_kv = recv_kv[local_dirs, slot_of]
    k_all = jnp.concatenate([k_own[:, None], nb_kv[:, :, 0]], axis=1).reshape(
        head_here, 5 * tile_tok, head_dim
    )
    v_all = jnp.concatenate([v_own[:, None], nb_kv[:, :, 1]], axis=1).reshape(
        head_here, 5 * tile_tok, head_dim
    )
    live_all = jnp.concatenate(
        [
            jnp.ones((head_here, tile_tok), jnp.float32),
            jnp.repeat(ahead_live[local_dirs], tile_tok, axis=1),
        ],
        axis=1,
    )
    key_count = 5 * tile_tok
    contract_rows = (((0,), (0,)), ((), ()))
    contract_cols = (((1,), (1,)), ((), ()))

    def query_side(inputs):
        q_rows, g_rows, lse_row, delta_row, k_rows, v_rows, live_row = inputs
        scores = (
            lax.dot_general(q_rows, k_rows, contract_cols, preferred_element_type=jnp.float32)
            * score_scale
        )
        attn_prob = jnp.exp(scores - lse_row[:, None]) * live_row[None, :]
        grad_prob = lax.dot_general(
            g_rows, v_rows, contract_cols, preferred_element_type=jnp.float32
        )
        grad_score = attn_prob * (grad_prob - delta_row[:, None])
        score_bf = grad_score.astype(jnp.bfloat16)
        prob_bf = attn_prob.astype(jnp.bfloat16)
        q_grad = jnp.dot(score_bf, k_rows, preferred_element_type=jnp.float32) * score_scale
        k_part = (
            lax.dot_general(score_bf, q_rows, contract_rows, preferred_element_type=jnp.float32)
            * score_scale
        )
        v_part = lax.dot_general(prob_bf, g_rows, contract_rows, preferred_element_type=jnp.float32)
        return (q_grad, k_part, v_part)

    q_grad, k_part, v_part = lax.map(
        query_side, (q_own, g_own, lse_own, delta_own, k_all, v_all, live_all)
    )
    k_self = k_part[:, :tile_tok]
    v_self = v_part[:, :tile_tok]
    part_bf = jnp.stack(
        [
            k_part[:, tile_tok:].reshape(head_here, 4, tile_tok, head_dim),
            v_part[:, tile_tok:].reshape(head_here, 4, tile_tok, head_dim),
        ],
        axis=2,
    ).astype(jnp.bfloat16)
    part_packs = [part_bf[head_of[direction], place_of[direction]] for direction in range(8)]
    returned = send_out(
        part_packs,
        lambda moving, offset_step: passed_along(moving, "sw", offset_step),
        lambda moving, offset_step: passed_along(moving, "sh", offset_step),
    )
    mine_parts = returned[local_dirs, slot_of]
    summed = jnp.sum(mine_parts.astype(jnp.float32), axis=1)
    k_total = k_self + summed[:, 0]
    v_total = v_self + summed[:, 1]

    def by_token(array):
        return jnp.transpose(array.astype(jnp.bfloat16), (1, 0, 2)).reshape(
            frames_all, tile_rows, tile_cols, head_here * head_dim
        )

    return (
        lax.all_to_all(by_token(q_grad), "tp", split_axis=0, concat_axis=3, tiled=True),
        lax.all_to_all(by_token(k_total), "tp", split_axis=0, concat_axis=3, tiled=True),
        lax.all_to_all(by_token(v_total), "tp", split_axis=0, concat_axis=3, tiled=True),
    )


def solution(mesh):
    return jax.shard_map(
        local,
        mesh=mesh,
        in_specs=(
            P("tp", "sh", "sw", None),
            P("tp", "sh", "sw", None),
            P("tp", "sh", "sw", None),
            P("tp", "sh", "sw", None),
            P("tp", "sh", "sw", None),
            P("tp", "sh", "sw", None),
            P(),
        ),
        out_specs=(P("tp", "sh", "sw", None), P("tp", "sh", "sw", None), P("tp", "sh", "sw", None)),
        check_vma=False,
    )
```

profile of v0, /device:TPU:4, one launch (start us, length us, event | category | flops | bytes accessed | tf_op | source)
XLA Modules:
  0.0 248.6 jit_solution(4305474917567733513)
XLA Ops:
  3.8 4.1 %reshape.753 = bf16[2,2,24576]{2,1,0:T(2,128)(2,1)} reshape(bf16[1536,1,8,8]{3,2,1,0:T(8,128)(2,1)S(1)} %bitcast.299) | data formatting | bytes 393216
  7.9 3.4 %all-to-all-start.1 = ((bf16[2,2,24576]{2,1,0:T(2,128)(2,1)}), bf16[2,2,24576]{2,1,0:T(2,128)(2,1)S(1)}, u32[]{:S(2)}, u32[]{:S(2)}) async-start(bf16[2,2,24576]{2,1,0:T(2,128)(2,1)} %reshape.753), calls=%async_computation.1 | async-start | bytes 393216 | tf_op jit(solution)/shard_map/all_to_all | solution.py:107
  26.8 4.1 %reshape.751 = bf16[2,2,24576]{2,1,0:T(2,128)(2,1)} reshape(bf16[1536,1,8,8]{3,2,1,0:T(8,128)(2,1)S(1)} %bitcast.300) | data formatting | bytes 393216
  30.9 4.1 %all-to-all-start.2 = ((bf16[2,2,24576]{2,1,0:T(2,128)(2,1)}), bf16[2,2,24576]{2,1,0:T(2,128)(2,1)}, u32[]{:S(2)}, u32[]{:S(2)}) async-start(bf16[2,2,24576]{2,1,0:T(2,128)(2,1)} %reshape.751), calls=%async_computation.2 | async-start | bytes 393216 | tf_op jit(solution)/shard_map/all_to_all | solution.py:108
  35.1 3.7 %reshape.754 = bf16[1536,1,8,8]{3,2,1,0:T(8,128)(2,1)S(1)} reshape(bf16[2,2,24576]{2,1,0:T(2,128)(2,1)S(1)} %all-to-all-done.1) | data formatting | bytes 393216
  45.6 4.5 %reshape.752 = bf16[1536,1,8,8]{3,2,1,0:T(8,128)(2,1)S(1)} reshape(bf16[2,2,24576]{2,1,0:T(2,128)(2,1)} %all-to-all-done.2) | data formatting | bytes 393216
  58.3 3.6 %collective-permute-start = (bf16[3,3,2,128,128]{4,3,2,1,0:T(8,128)(2,1)S(1)}, bf16[3,3,2,128,128]{4,3,2,1,0:T(8,128)(2,1)S(1)}, u32[]{:S(2)}, u32[]{:S(2)}) collective-permute-start(bf16[3,3,2,128,128]{4,3,2,1,0:T(8,128)(2,1)S(1)} %pad_maximum_fusion.4), channel_id=1, source_target_pairs={{0,8},{8,16},{16,24},{1,9},{9,17},{17,25},{2,10},{10,18},{18,26},{... | collective-permute-start | bytes 1769480 | tf_op jit(solution)/shard_map/ppermute | solution.py:12
  65.1 9.3 %collective-permute-done = bf16[3,3,2,128,128]{4,3,2,1,0:T(8,128)(2,1)S(1)} collective-permute-done((bf16[3,3,2,128,128]{4,3,2,1,0:T(8,128)(2,1)S(1)}, bf16[3,3,2,128,128]{4,3,2,1,0:T(8,128)(2,1)S(1)}, u32[]{:S(2)}, u32[]{:S(2)}) %collective-permute-start) | collective-permute-done | bytes 589856 | tf_op jit(solution)/shard_map/ppermute | solution.py:12
  74.4 4.5 %collective-permute-done.1 = bf16[3,3,2,128,128]{4,3,2,1,0:T(8,128)(2,1)S(1)} collective-permute-done((bf16[3,3,2,128,128]{4,3,2,1,0:T(8,128)(2,1)S(1)}, bf16[3,3,2,128,128]{4,3,2,1,0:T(8,128)(2,1)S(1)}, u32[]{:S(2)}, u32[]{:S(2)}) %collective-permute-start.1) | collective-permute-done | bytes 589856 | tf_op jit(solution)/shard_map/ppermute | solution.py:12
  83.3 7.0 %collective-permute-done.2 = bf16[3,3,2,128,128]{4,3,2,1,0:T(8,128)(2,1)S(1)} collective-permute-done((bf16[3,3,2,128,128]{4,3,2,1,0:T(8,128)(2,1)S(1)}, bf16[3,3,2,128,128]{4,3,2,1,0:T(8,128)(2,1)S(1)}, u32[]{:S(2)}, u32[]{:S(2)}) %collective-permute-start.2) | collective-permute-done | bytes 589856 | tf_op jit(solution)/shard_map/ppermute | solution.py:12
  101.6 4.2 %reshape.749 = bf16[2,2,24576]{2,1,0:T(2,128)(2,1)} reshape(bf16[1536,1,8,8]{3,2,1,0:T(8,128)(2,1)S(1)} %bitcast.301) | data formatting | bytes 393216
  105.8 4.1 %all-to-all-start = ((bf16[2,2,24576]{2,1,0:T(2,128)(2,1)}), bf16[2,2,24576]{2,1,0:T(2,128)(2,1)}, u32[]{:S(2)}, u32[]{:S(2)}) async-start(bf16[2,2,24576]{2,1,0:T(2,128)(2,1)} %reshape.749), calls=%async_computation | async-start | bytes 393216 | tf_op jit(solution)/shard_map/all_to_all | solution.py:106
  114.3 4.2 %reshape.757 = bf16[2,2,24576]{2,1,0:T(2,128)(2,1)} reshape(bf16[1536,1,8,8]{3,2,1,0:T(8,128)(2,1)S(1)} %bitcast.302) | data formatting | bytes 393216
  118.6 4.1 %all-to-all-start.4 = ((bf16[2,2,24576]{2,1,0:T(2,128)(2,1)}), bf16[2,2,24576]{2,1,0:T(2,128)(2,1)}, u32[]{:S(2)}, u32[]{:S(2)}) async-start(bf16[2,2,24576]{2,1,0:T(2,128)(2,1)} %reshape.757), calls=%async_computation.4 | async-start | bytes 393216 | tf_op jit(solution)/shard_map/all_to_all | solution.py:109
  128.3 4.5 %reshape.750 = bf16[1536,1,8,8]{3,2,1,0:T(8,128)(2,1)S(1)} reshape(bf16[2,2,24576]{2,1,0:T(2,128)(2,1)} %all-to-all-done) | data formatting | bytes 393216
  137.1 4.5 %reshape.758 = bf16[1536,1,8,8]{3,2,1,0:T(8,128)(2,1)S(1)} reshape(bf16[2,2,24576]{2,1,0:T(2,128)(2,1)} %all-to-all-done.4) | data formatting | bytes 393216
  158.3 29.2 %while.14 = (s32[]{:T(128)}, bf16[6,128,128]{2,1,0:T(8,128)(2,1)S(1)}, f32[6,640,128]{2,1,0:T(8,128)}, f32[6,640,128]{2,1,0:T(8,128)}, bf16[6,128,128]{2,1,0:T(8...) while((s32[]{:T(128)}, ...), condition=%wide.region_6.8_spmd, body=%wide.region_5.7_spmd.sunk | while | flops 105529344 | bytes 2835589 | solution.py:177
  203.7 6.1 %collective-permute-done.5 = bf16[3,3,2,128,128]{4,3,2,1,0:T(8,128)(2,1)} collective-permute-done((bf16[3,3,2,128,128]{4,3,2,1,0:T(8,128)(2,1)}, bf16[3,3,2,128,128]{4,3,2,1,0:T(8,128)(2,1)}, u32[]{:S(2)}, u32[]{:S(2)}) %collective-permute-start.5) | collective-permute-done | bytes 589856 | tf_op jit(solution)/shard_map/ppermute | solution.py:12
  211.0 3.5 %collective-permute-start.7 = (bf16[3,3,2,128,128]{4,3,2,1,0:T(8,128)(2,1)S(1)}, bf16[3,3,2,128,128]{4,3,2,1,0:T(8,128)(2,1)S(1)}, u32[]{:S(2)}, u32[]{:S(2)}) collective-permute-start(bf16[3,3,2,128,128]{4,3,2,1,0:T(8,128)(2,1)S(1)} %pad_maximum_fusion.11), channel_id=1, source_target_pairs={{0,8},{8,16},{16,24},{1,9},{9,17},{17,25},{2,10},{10,18},{18,26},{... | collective-permute-start | bytes 1769480 | tf_op jit(solution)/shard_map/ppermute | solution.py:12
  217.0 3.4 %all-to-all-start.6 = ((bf16[2,8,8,768]{3,2,1,0:T(8,128)(2,1)}), bf16[2,8,8,768]{3,2,1,0:T(8,128)(2,1)S(1)}, u32[]{:S(2)}, u32[]{:S(2)}) async-start(bf16[2,8,8,768]{3,2,1,0:T(8,128)(2,1)} %reshape.555), calls=%async_computation.6 | async-start | bytes 393216 | tf_op jit(solution)/shard_map/all_to_all | solution.py:206
  221.9 4.6 %collective-permute-done.6 = bf16[3,3,2,128,128]{4,3,2,1,0:T(8,128)(2,1)} collective-permute-done((bf16[3,3,2,128,128]{4,3,2,1,0:T(8,128)(2,1)S(1)}, bf16[3,3,2,128,128]{4,3,2,1,0:T(8,128)(2,1)}, u32[]{:S(2)}, u32[]{:S(2)}) %collective-permute-start.6) | collective-permute-done | bytes 589856 | tf_op jit(solution)/shard_map/ppermute | solution.py:12
  231.4 3.4 %all-to-all-start.8 = ((bf16[2,8,8,768]{3,2,1,0:T(8,128)(2,1)}), bf16[2,8,8,768]{3,2,1,0:T(8,128)(2,1)S(1)}, u32[]{:S(2)}, u32[]{:S(2)}) async-start(bf16[2,8,8,768]{3,2,1,0:T(8,128)(2,1)} %reshape.557), calls=%async_computation.8 | async-start | bytes 393216 | tf_op jit(solution)/shard_map/all_to_all | solution.py:208
  235.9 3.7 %all-to-all-done.8 = bf16[2,8,8,768]{3,2,1,0:T(8,128)(2,1)S(1)} async-done(((bf16[2,8,8,768]{3,2,1,0:T(8,128)(2,1)}), bf16[2,8,8,768]{3,2,1,0:T(8,128)(2,1)S(1)}, u32[]{:S(2)}, u32[]{:S(2)}) %all-to-all-start.8) | async-done | bytes 196640 | tf_op jit(solution)/shard_map/all_to_all | solution.py:208
  239.7 3.4 %all-to-all-start.7 = ((bf16[2,8,8,768]{3,2,1,0:T(8,128)(2,1)}), bf16[2,8,8,768]{3,2,1,0:T(8,128)(2,1)S(1)}, u32[]{:S(2)}, u32[]{:S(2)}) async-start(bf16[2,8,8,768]{3,2,1,0:T(8,128)(2,1)} %reshape.556), calls=%async_computation.7 | async-start | bytes 393216 | tf_op jit(solution)/shard_map/all_to_all | solution.py:207
  (287 shorter events, 144.5 us)
Async XLA Ops:
  3.8 20.8 %copy-start.4 = (bf16[1,8,8,1536]{3,2,1,0:T(8,128)(2,1)S(1)}, bf16[1,8,8,1536]{3,2,1,0:T(8,128)(2,1)}, u32[]{:S(2)}) copy-start(bf16[1,8,8,1536]{3,2,1,0:T(8,128)(2,1)} %param.14) | copy-start | bytes 589828
  7.9 23.1 %all-to-all-start.1 = ((bf16[2,2,24576]{2,1,0:T(2,128)(2,1)}), bf16[2,2,24576]{2,1,0:T(2,128)(2,1)S(1)}, u32[]{:S(2)}, u32[]{:S(2)}) async-start(bf16[2,2,24576]{2,1,0:T(2,128)(2,1)} %reshape.753), calls=%async_computation.1 | async-start | bytes 393216 | tf_op jit(solution)/shard_map/all_to_all | solution.py:107
  12.8 9.5 %copy-start.21 = (s32[3]{0:T(128)}, s32[3]{0:T(128)S(1)}, u32[]{:S(2)}) copy-start(s32[3]{0:T(128)S(1)} %get-tuple-element.186) | copy-start | bytes 40
  12.8 9.6 %copy-start.23 = (s32[3]{0:T(128)}, s32[3]{0:T(128)S(1)}, u32[]{:S(2)}) copy-start(s32[3]{0:T(128)S(1)} %get-tuple-element.187) | copy-start | bytes 40
  30.9 11.3 %all-to-all-start.2 = ((bf16[2,2,24576]{2,1,0:T(2,128)(2,1)}), bf16[2,2,24576]{2,1,0:T(2,128)(2,1)}, u32[]{:S(2)}, u32[]{:S(2)}) async-start(bf16[2,2,24576]{2,1,0:T(2,128)(2,1)} %reshape.751), calls=%async_computation.2 | async-start | bytes 393216 | tf_op jit(solution)/shard_map/all_to_all | solution.py:108
  42.3 52.1 %all-to-all-start.3 = ((f32[2,1,384]{2,1,0:T(1,128)}), f32[2,1,384]{2,1,0:T(1,128)S(1)}, u32[]{:S(2)}, u32[]{:S(2)}) async-start(f32[2,1,384]{2,1,0:T(1,128)} %reshape.755), calls=%async_computation.3 | async-start | bytes 6144 | tf_op jit(solution)/shard_map/all_to_all | solution.py:112
  58.3 16.1 %collective-permute-start = (bf16[3,3,2,128,128]{4,3,2,1,0:T(8,128)(2,1)S(1)}, bf16[3,3,2,128,128]{4,3,2,1,0:T(8,128)(2,1)S(1)}, u32[]{:S(2)}, u32[]{:S(2)}) collective-permute-start(bf16[3,3,2,128,128]{4,3,2,1,0:T(8,128)(2,1)S(1)} %pad_maximum_fusion.4), channel_id=1, source_target_pairs={{0,8},{8,16},{16,24},{1,9},{9,17},{17,25},{2,10},{10,18},{18,26},{... | collective-permute-start | bytes 1769480 | tf_op jit(solution)/shard_map/ppermute | solution.py:12
  62.3 16.6 %collective-permute-start.1 = (bf16[3,3,2,128,128]{4,3,2,1,0:T(8,128)(2,1)S(1)}, bf16[3,3,2,128,128]{4,3,2,1,0:T(8,128)(2,1)S(1)}, u32[]{:S(2)}, u32[]{:S(2)}) collective-permute-start(bf16[3,3,2,128,128]{4,3,2,1,0:T(8,128)(2,1)S(1)} %pad_maximum_fusion.5), channel_id=1, source_target_pairs={{8,0},{16,8},{24,16},{9,1},{17,9},{25,17},{10,2},{18,10},{26,18},{... | collective-permute-start | bytes 1769480 | tf_op jit(solution)/shard_map/ppermute | solution.py:12
  64.4 16.5 %copy-start.15 = (s32[24]{0:T(128)S(1)}, s32[24]{0:T(128)}, u32[]{:S(2)}) copy-start(s32[24]{0:T(128)} %reshape.632) | copy-start | bytes 292
  79.0 11.2 %collective-permute-start.2 = (bf16[3,3,2,128,128]{4,3,2,1,0:T(8,128)(2,1)S(1)}, bf16[3,3,2,128,128]{4,3,2,1,0:T(8,128)(2,1)S(1)}, u32[]{:S(2)}, u32[]{:S(2)}) collective-permute-start(bf16[3,3,2,128,128]{4,3,2,1,0:T(8,128)(2,1)S(1)} %pad_maximum_fusion.6), channel_id=1, source_target_pairs={{0,2},{2,4},{4,6},{1,3},{3,5},{5,7},{8,10},{10,12},{12,14},{9,11},... | collective-permute-start | bytes 1769480 | tf_op jit(solution)/shard_map/ppermute | solution.py:12
  82.6 15.3 %copy-start.22 = (s32[3]{0:T(128)S(1)}, s32[3]{0:T(128)}, u32[]{:S(2)}) copy-start(s32[3]{0:T(128)} %get-tuple-element.130) | copy-start | bytes 40
  82.6 15.3 %copy-start.24 = (s32[3]{0:T(128)S(1)}, s32[3]{0:T(128)}, u32[]{:S(2)}) copy-start(s32[3]{0:T(128)} %copy-done.23) | copy-start | bytes 40
  92.5 52.7 %collective-permute-start.3 = (bf16[3,3,2,128,128]{4,3,2,1,0:T(8,128)(2,1)}, bf16[3,3,2,128,128]{4,3,2,1,0:T(8,128)(2,1)}, u32[]{:S(2)}, u32[]{:S(2)}) collective-permute-start(bf16[3,3,2,128,128]{4,3,2,1,0:T(8,128)(2,1)} %pad_maximum_fusion.7), channel_id=1, source_target_pairs={{2,0},{4,2},{6,4},{3,1},{5,3},{7,5},{10,8},{12,10},{14,12},{11,9},... | collective-permute-start | bytes 1769480 | tf_op jit(solution)/shard_map/ppermute | solution.py:12
  94.5 11.3 %all-to-all-start.5 = ((f32[2,1,384]{2,1,0:T(1,128)}), f32[2,1,384]{2,1,0:T(1,128)S(1)}, u32[]{:S(2)}, u32[]{:S(2)}) async-start(f32[2,1,384]{2,1,0:T(1,128)} %reshape.759), calls=%async_computation.5 | async-start | bytes 6144 | tf_op jit(solution)/shard_map/all_to_all | solution.py:113
  105.8 12.8 %all-to-all-start = ((bf16[2,2,24576]{2,1,0:T(2,128)(2,1)}), bf16[2,2,24576]{2,1,0:T(2,128)(2,1)}, u32[]{:S(2)}, u32[]{:S(2)}) async-start(bf16[2,2,24576]{2,1,0:T(2,128)(2,1)} %reshape.749), calls=%async_computation | async-start | bytes 393216 | tf_op jit(solution)/shard_map/all_to_all | solution.py:106
  114.3 9.6 %copy-start.14 = (s32[6,4,1]{0,1,2:T(4,128)S(1)}, s32[6,4,1]{0,1,2:T(4,128)}, u32[]{:S(2)}) copy-start(s32[6,4,1]{0,1,2:T(4,128)} %fusion.43) | copy-start | bytes 292
  118.6 18.5 %all-to-all-start.4 = ((bf16[2,2,24576]{2,1,0:T(2,128)(2,1)}), bf16[2,2,24576]{2,1,0:T(2,128)(2,1)}, u32[]{:S(2)}, u32[]{:S(2)}) async-start(bf16[2,2,24576]{2,1,0:T(2,128)(2,1)} %reshape.757), calls=%async_computation.4 | async-start | bytes 393216 | tf_op jit(solution)/shard_map/all_to_all | solution.py:109
  193.0 10.7 %collective-permute-start.4 = (bf16[3,3,2,128,128]{4,3,2,1,0:T(8,128)(2,1)S(1)}, bf16[3,3,2,128,128]{4,3,2,1,0:T(8,128)(2,1)S(1)}, u32[]{:S(2)}, u32[]{:S(2)}) collective-permute-start(bf16[3,3,2,128,128]{4,3,2,1,0:T(8,128)(2,1)S(1)} %pad_maximum_fusion.8), channel_id=1, source_target_pairs={{2,0},{4,2},{6,4},{3,1},{5,3},{7,5},{10,8},{12,10},{14,12},{11,9},... | collective-permute-start | bytes 1769480 | tf_op jit(solution)/shard_map/ppermute | solution.py:12
  198.3 11.5 %collective-permute-start.5 = (bf16[3,3,2,128,128]{4,3,2,1,0:T(8,128)(2,1)}, bf16[3,3,2,128,128]{4,3,2,1,0:T(8,128)(2,1)}, u32[]{:S(2)}, u32[]{:S(2)}) collective-permute-start(bf16[3,3,2,128,128]{4,3,2,1,0:T(8,128)(2,1)} %pad_maximum_fusion.9), channel_id=1, source_target_pairs={{0,2},{2,4},{4,6},{1,3},{3,5},{5,7},{8,10},{10,12},{12,14},{9,11},... | collective-permute-start | bytes 1769480 | tf_op jit(solution)/shard_map/ppermute | solution.py:12
  211.0 10.8 %collective-permute-start.7 = (bf16[3,3,2,128,128]{4,3,2,1,0:T(8,128)(2,1)S(1)}, bf16[3,3,2,128,128]{4,3,2,1,0:T(8,128)(2,1)S(1)}, u32[]{:S(2)}, u32[]{:S(2)}) collective-permute-start(bf16[3,3,2,128,128]{4,3,2,1,0:T(8,128)(2,1)S(1)} %pad_maximum_fusion.11), channel_id=1, source_target_pairs={{0,8},{8,16},{16,24},{1,9},{9,17},{17,25},{2,10},{10,18},{18,26},{... | collective-permute-start | bytes 1769480 | tf_op jit(solution)/shard_map/ppermute | solution.py:12
  214.6 11.9 %collective-permute-start.6 = (bf16[3,3,2,128,128]{4,3,2,1,0:T(8,128)(2,1)S(1)}, bf16[3,3,2,128,128]{4,3,2,1,0:T(8,128)(2,1)}, u32[]{:S(2)}, u32[]{:S(2)}) collective-permute-start(bf16[3,3,2,128,128]{4,3,2,1,0:T(8,128)(2,1)S(1)} %pad_maximum_fusion.10), channel_id=1, source_target_pairs={{8,0},{16,8},{24,16},{9,1},{17,9},{25,17},{10,2},{18,10},{26,18},{... | collective-permute-start | bytes 1769480 | tf_op jit(solution)/shard_map/ppermute | solution.py:12
  217.0 14.4 %all-to-all-start.6 = ((bf16[2,8,8,768]{3,2,1,0:T(8,128)(2,1)}), bf16[2,8,8,768]{3,2,1,0:T(8,128)(2,1)S(1)}, u32[]{:S(2)}, u32[]{:S(2)}) async-start(bf16[2,8,8,768]{3,2,1,0:T(8,128)(2,1)} %reshape.555), calls=%async_computation.6 | async-start | bytes 393216 | tf_op jit(solution)/shard_map/all_to_all | solution.py:206
  231.4 8.2 %all-to-all-start.8 = ((bf16[2,8,8,768]{3,2,1,0:T(8,128)(2,1)}), bf16[2,8,8,768]{3,2,1,0:T(8,128)(2,1)S(1)}, u32[]{:S(2)}, u32[]{:S(2)}) async-start(bf16[2,8,8,768]{3,2,1,0:T(8,128)(2,1)} %reshape.557), calls=%async_computation.8 | async-start | bytes 393216 | tf_op jit(solution)/shard_map/all_to_all | solution.py:208
  239.7 8.2 %all-to-all-start.7 = ((bf16[2,8,8,768]{3,2,1,0:T(8,128)(2,1)}), bf16[2,8,8,768]{3,2,1,0:T(8,128)(2,1)S(1)}, u32[]{:S(2)}, u32[]{:S(2)}) async-start(bf16[2,8,8,768]{3,2,1,0:T(8,128)(2,1)} %reshape.556), calls=%async_computation.7 | async-start | bytes 393216 | tf_op jit(solution)/shard_map/all_to_all | solution.py:207
  (31 other events, 155.5 us)
where the time goes:
time: 252 us; the launch traced here: 249 us
  local copies, waits for them, and re-layouts  107 us (42%)
  starting transfers between devices  51 us (20%)
  waiting for transfers between devices  40.1 us (16%)
  matrix products  24.6 us (10%)
  other arithmetic  24.4 us (10%)
    unnamed x101, local copies, waits for them, and re-layouts  58.1 us
    ppermute x8, waiting for transfers between devices, passed_along(): return lax.ppermute(block, axis, route)  32.9 us
    ppermute x8, starting transfers between devices, passed_along(): return lax.ppermute(block, axis, route)  18.3 us
    dot_general x6, matrix products, query_side(): lax.dot_general(score_bf, q_rows, contract_rows, preferred_element_type=j...  10.3 us
    concatenate x8, other arithmetic, local(): part_bf[head_of[direction], place_of[direction]]  6.04 us
    dot_general x6, matrix products, query_side(): lax.dot_general(q_rows, k_rows, contract_cols, preferred_element_type=jnp...  5.93 us
    dot_general x6, matrix products, query_side(): lax.dot_general(prob_bf, g_rows, contract_rows, preferred_element_type=jn...  5.82 us
    gather x8, local copies, waits for them, and re-layouts, local(): jnp.take(kv_own, head_of[direction], axis=0)  5.17 us
  transfers between devices with their start and end apart: 17, of which 8 were waited for; matrix products, arithmetic and copies ran while one was open for 40% of the time, Pallas kernels for 0%

commit v1 on v0

v1 whole, which is shorter than its diff:
```python
import functools

import jax
import jax.numpy as jnp
from jax import lax
from jax.experimental import pallas as pl
from jax.experimental.pallas import tpu as pltpu
from jax.sharding import PartitionSpec as P

E_OF = (1, 7, 4, 0, 3, 2, 8, 5)
BF = jnp.bfloat16
F32 = jnp.float32
NT = (((1,), (1,)), ((), ()))
TN = (((0,), (0,)), ((), ()))


def kernel(
    n_sh, n_sw, half, hd,
    q_ref, k_ref, v_ref, g_ref, o_ref, lse_ref, wd_ref,
    dq_out, dk_out, dv_out,
    zb00, zb01, zb10, zb11, kv0, kv1, qg, pieces, packed, stats,
    rs00, rs01, rs02, rs10, rs11, rs12, dqs, dkp, own_kv, own_q,
    zsend, zback, xsend, xback, head_of, rank_of, member_of, flat_of,
    zs, zr, zts, ztr, xs, xr, ws, wr, wts, wtr, rs, rr, rzs, rzr, rxs, rxr,
):
    row = lax.axis_index("sh")
    col = lax.axis_index("sw")
    part = lax.axis_index("tp")
    zb = ((zb00, zb01), (zb10, zb11))
    kv = (kv0, kv1)
    rsw = ((rs00, rs01, rs02), (rs10, rs11, rs12))
    third = half // 2
    tok = q_ref.shape[0]
    scale = hd ** -0.5
    row_ok = lambda step: (row + step >= 0) & (row + step < n_sh)
    col_ok = lambda step: (col + step >= 0) & (col + step < n_sw)
    row_step = (0, -1, 1)
    col_step = (-1, 1)

    def remote(src, dst, ssem, rsem, device):
        return pltpu.make_async_remote_copy(
            src_ref=src, dst_ref=dst, send_sem=ssem, recv_sem=rsem,
            device_id=device, device_id_type=pl.DeviceIdType.MESH,
        )

    def copy_z(run, i):
        return remote(qg.at[run], zb[run][i], zs.at[run, i], zr.at[run, i], {"sh": row + 2 * i - 1})

    def copy_zstat(i):
        return remote(stats.at[6], stats.at[7 + i], zts.at[i], ztr.at[i], {"sh": row + 2 * i - 1})

    def copy_x(run):
        src = kv[run].at[:, :, pl.ds(0, tok)]
        dst = kv[run].at[:, :, pl.ds(tok, tok)]
        return remote(src, dst, xs.at[run], xr.at[run], {"tp": 1 - part})

    def copy_w(run, c, i):
        e = c * 3 + i
        return remote(packed.at[run, e], pieces.at[run, e], ws.at[run, e], wr.at[run, e], {"sw": col + col_step[c]})

    def copy_wstat(c, i):
        e = c * 3 + i
        return remote(stats.at[6 + i], stats.at[e], wts.at[e], wtr.at[e], {"sw": col + col_step[c]})

    def copy_back(run, c, i):
        e = c * 3 + i
        return remote(dqs.at[run * 9 + e], rsw[run][i].at[c], rs.at[run, e], rr.at[run, e], {"sw": col - col_step[c]})

    def copy_zback(run, i):
        return remote(zsend.at[run, i], zback.at[run, i], rzs.at[run, i], rzr.at[run, i], {"sh": row - (2 * i - 1)})

    def copy_xback(run):
        return remote(xsend.at[run], xback.at[run], rxs.at[run], rxr.at[run], {"tp": 1 - part})

    barrier = pltpu.get_barrier_semaphore()
    pl.semaphore_signal(barrier, inc=1, device_id={"tp": 1 - part}, device_id_type=pl.DeviceIdType.MESH)
    for step in (-1, 1):
        @pl.when(row_ok(step))
        def _():
            pl.semaphore_signal(barrier, inc=1, device_id={"sh": row + step}, device_id_type=pl.DeviceIdType.MESH)

        @pl.when(col_ok(step))
        def _():
            pl.semaphore_signal(barrier, inc=1, device_id={"sw": col + step}, device_id_type=pl.DeviceIdType.MESH)
    for run in (0, 1):
        for h in range(half):
            cols = slice((run * half + h) * hd, (run * half + h + 1) * hd)
            qg[run, 0, h] = q_ref[:, cols]
            qg[run, 1, h] = g_ref[:, cols]
            kv[run][0, h, :tok] = k_ref[:, cols]
            kv[run][1, h, :tok] = v_ref[:, cols]
    count = 1
    for step in (-1, 1):
        count = count + row_ok(step).astype(jnp.int32) + col_ok(step).astype(jnp.int32)
    pl.semaphore_wait(barrier, count)

    for run in (0, 1):
        for i in (0, 1):
            @pl.when(row_ok(2 * i - 1))
            def _():
                copy_z(run, i).start()
        copy_x(run).start()

    for run in (0, 1):
        dirs = [[wd_ref[run * half + h, j] for j in range(4)] for h in range(half)]
        flat = [[jnp.int32(0) for j in range(4)] for h in range(half)]
        for d in range(8):
            e = E_OF[d]
            seen = jnp.int32(0)
            heads = [jnp.int32(0) for _ in range(third)]
            for h in range(half):
                named = [(dirs[h][j] == d).astype(jnp.int32) for j in range(4)]
                member = named[0] + named[1] + named[2] + named[3]
                rank = jnp.minimum(seen, third - 1)
                rank_of[(run * 9 + e) * half + h] = rank
                member_of[(run * 9 + e) * half + h] = member
                at = (run * 9 + e) * third + rank
                for j in range(4):
                    flat[h][j] = flat[h][j] + named[j] * at
                for s in range(third):
                    heads[s] = heads[s] + member * (seen == s).astype(jnp.int32) * h
                seen = seen + member
            for s in range(third):
                head_of[(run * 9 + e) * third + s] = heads[s]
        for h in range(half):
            for j in range(4):
                flat_of[(run * half + h) * 4 + j] = flat[h][j]

    def pack(run, c, i):
        e = c * 3 + i
        for s in range(third):
            h = head_of[(run * 9 + e) * third + s]
            for a in (0, 1):
                block = qg[run, a, h] if i == 0 else zb[run][i - 1][a, h]
                if c == 2:
                    pieces[run, e, s, a] = block
                else:
                    packed[run, e, s, a] = block

    for run in (0, 1):
        for c in (0, 1):
            @pl.when(col_ok(col_step[c]))
            def _():
                pack(run, c, 0)
                copy_w(run, c, 0).start()

    lane = lax.broadcasted_iota(jnp.int32, (tok, hd), 1)
    table = jnp.zeros((tok, hd), F32)
    for run in (0, 1):
        for h in range(half):
            at = run * half + h
            cols = slice(at * hd, (at + 1) * hd)
            delta = jnp.sum(g_ref[:, cols].astype(F32) * o_ref[:, cols].astype(F32), axis=1, keepdims=True)
            table = jnp.where(lane == run * 16 + h, lse_ref[:, at:at + 1], table)
            table = jnp.where(lane == run * 16 + 8 + h, delta, table)
    square = jnp.concatenate([table, jnp.zeros((hd - tok, hd), F32)], axis=0) if tok < hd else table
    stats[6] = square.T[:32, :]
    for i in (0, 1):
        @pl.when(row_ok(2 * i - 1))
        def _():
            copy_zstat(i).start()
    for c in (0, 1):
        @pl.when(col_ok(col_step[c]))
        def _():
            copy_wstat(c, 0).start()

    def clear(e, carry):
        i = lax.rem(e, 3)
        c = lax.div(e, 3)
        r_step = jnp.where(i == 0, 0, 2 * i - 3)
        c_step = jnp.where(c == 2, 0, 2 * c - 1)
        live = row_ok(-r_step) & col_ok(-c_step)

        @pl.when(jnp.logical_not(live))
        def _():
            for run in (0, 1):
                for s in range(third):
                    dkp[(run * 9 + e) * third + s] = jnp.zeros(dkp.shape[1:], BF)
        return carry

    lax.fori_loop(0, 9, clear, 0)
    for c in (0, 1):
        @pl.when(jnp.logical_not(col_ok(col_step[c])))
        def _():
            for run in (0, 1):
                for i in range(3):
                    rsw[run][i][c] = jnp.zeros(rs00.shape[1:], BF)
    for i in (0, 1):
        @pl.when(jnp.logical_not(row_ok(2 * i - 1)))
        def _():
            for run in (0, 1):
                zback[run, i] = jnp.zeros(zback.shape[2:], BF)

    sub = lax.broadcasted_iota(jnp.int32, (8, hd), 0)

    def one(run, h, q, g, stat):
        keys = kv[run][0, h]
        vals = kv[run][1, h]
        pick = sub == h
        lse = jnp.sum(jnp.where(pick, stat[run * 16:run * 16 + 8], 0.0), axis=0, keepdims=True)[:, :tok]
        delta = jnp.sum(jnp.where(pick, stat[run * 16 + 8:run * 16 + 16], 0.0), axis=0, keepdims=True)[:, :tok]
        scores = lax.dot_general(keys, q, NT, preferred_element_type=F32)
        prob = jnp.exp(scores * scale - lse)
        grad_prob = lax.dot_general(vals, g, NT, preferred_element_type=F32)
        score_bf = (prob * (grad_prob - delta)).astype(BF)
        prob_bf = prob.astype(BF)
        dv = jnp.dot(prob_bf, g, preferred_element_type=F32)
        dk = jnp.dot(score_bf, q, preferred_element_type=F32) * scale
        dq = lax.dot_general(score_bf, keys, TN, preferred_element_type=F32) * scale
        return dq, dk, dv

    def own(run):
        def body(t, carry):
            stat = stats[6]
            for u in range(3):
                h = t * 3 + u
                dq, dk, dv = one(run, h, qg[run, 0, h], qg[run, 1, h], stat)
                own_q[run * half + h] = dq
                own_kv[run * half + h, 0] = dk
                own_kv[run * half + h, 1] = dv
            return carry

        lax.fori_loop(0, half // 3, body, 0)

    def group(run, e):
        stat = stats[e]
        for s in range(third):
            h = head_of[(run * 9 + e) * third + s]
            dq, dk, dv = one(run, h, pieces[run, e, s, 0], pieces[run, e, s, 1], stat)
            dqs[run * 9 + e, s] = dq.astype(BF)
            dkp[(run * 9 + e) * third + s, 0] = dk.astype(BF)
            dkp[(run * 9 + e) * third + s, 1] = dv.astype(BF)

    def from_side(run, c, i):
        @pl.when(row_ok(-row_step[i]) & col_ok(-col_step[c]))
        def _():
            copy_w(run, c, i).wait_recv()
            if run == 0:
                copy_wstat(c, i).wait_recv()
            group(run, c * 3 + i)
            copy_back(run, c, i).start()

    def relay(run):
        for i in (1, 2):
            @pl.when(row_ok(-row_step[i]))
            def _():
                copy_z(run, i - 1).wait_recv()
                if run == 0:
                    copy_zstat(i - 1).wait_recv()
                for c in (0, 1):
                    @pl.when(col_ok(col_step[c]))
                    def _():
                        pack(run, c, i)
                        copy_w(run, c, i).start()
                        if run == 0:
                            copy_wstat(c, i).start()
                pack(run, 2, i)

    def from_rows(run):
        for i in (1, 2):
            @pl.when(row_ok(-row_step[i]))
            def _():
                group(run, 6 + i)

    def wait_back(run, i):
        for c in (0, 1):
            @pl.when(row_ok(-row_step[i]) & col_ok(col_step[c]))
            def _():
                copy_back(run, c, i).wait_recv()

    def gathered(run, i, h, total):
        for c in (0, 1, 2):
            if c == 2 and i == 0:
                continue
            e = c * 3 + i
            rank = rank_of[(run * 9 + e) * half + h]
            held = dqs[run * 9 + e, rank] if c == 2 else rsw[run][i][c, rank]
            block = held.astype(F32) * member_of[(run * 9 + e) * half + h].astype(F32)
            total = block if total is None else total + block
        return total

    def turn(run):
        for i in (1, 2):
            @pl.when(row_ok(-row_step[i]))
            def _():
                wait_back(run, i)

                def body(h, carry):
                    zsend[run, i - 1, h] = gathered(run, i, h, None).astype(BF)
                    return carry

                lax.fori_loop(0, half, body, 0)
                copy_zback(run, i - 1).start()

    def total_kv(run, h, rows, a):
        total = own_kv[run * half + h, a, rows]
        for j in range(4):
            at = flat_of[(run * half + h) * 4 + j]
            total = total + dkp[at, a, rows].astype(F32)
        return total

    def to_partner(run):
        def body(h, carry):
            for a in (0, 1):
                xsend[run, a, h] = total_kv(run, h, slice(tok, 2 * tok), a).astype(BF)
            return carry

        lax.fori_loop(0, half, body, 0)
        copy_xback(run).start()

    def finish_kv(run):
        copy_xback(run).wait_recv()

        def body(h, carry):
            cols = pl.ds(pl.multiple_of((run * half + h) * hd, hd), hd)
            for a, out in ((0, dk_out), (1, dv_out)):
                total = total_kv(run, h, slice(0, tok), a) + xback[run, a, h].astype(F32)
                out[:, cols] = total.astype(BF)
            return carry

        lax.fori_loop(0, half, body, 0)

    def finish_q(run):
        wait_back(run, 0)
        for i in (0, 1):
            @pl.when(row_ok(2 * i - 1))
            def _():
                copy_zback(run, i).wait_recv()

        def body(h, carry):
            cols = pl.ds(pl.multiple_of((run * half + h) * hd, hd), hd)
            total = gathered(run, 0, h, own_q[run * half + h])
            total = total + zback[run, 0, h].astype(F32) + zback[run, 1, h].astype(F32)
            dq_out[:, cols] = total.astype(BF)
            return carry

        lax.fori_loop(0, half, body, 0)

    copy_x(0).wait_recv()
    own(0)
    relay(0)
    from_rows(0)
    from_side(0, 0, 0)
    from_side(0, 1, 0)
    copy_x(1).wait_recv()
    relay(1)
    for c in (0, 1):
        for i in (1, 2):
            from_side(0, c, i)
    from_rows(1)
    to_partner(0)
    turn(0)
    own(1)
    from_side(1, 0, 0)
    from_side(1, 1, 0)
    for c in (0, 1):
        for i in (1, 2):
            from_side(1, c, i)
    to_partner(1)
    turn(1)
    finish_kv(0)
    finish_q(0)
    finish_kv(1)
    finish_q(1)

    for run in (0, 1):
        copy_x(run).wait_send()
        copy_xback(run).wait_send()
        for i in (0, 1):
            @pl.when(row_ok(2 * i - 1))
            def _():
                copy_z(run, i).wait_send()
                if run == 0:
                    copy_zstat(i).wait_send()

            @pl.when(row_ok(1 - 2 * i))
            def _():
                copy_zback(run, i).wait_send()
        for c in (0, 1):
            for i in range(3):
                @pl.when(row_ok(-row_step[i]) & col_ok(col_step[c]))
                def _():
                    copy_w(run, c, i).wait_send()
                    if run == 0:
                        copy_wstat(c, i).wait_send()

                @pl.when(row_ok(-row_step[i]) & col_ok(-col_step[c]))
                def _():
                    copy_back(run, c, i).wait_send()


def local(n_sh, n_sw, queries, keys, values, attn_out, attn_grad, log_sum, window_dirs):
    shape = queries.shape
    tok = shape[0] * shape[1] * shape[2]
    cols = shape[3]
    heads = log_sum.shape[3]
    half = heads // 2
    third = half // 2
    hd = cols // heads
    flat = lambda array: array.reshape(tok, array.shape[3])
    vmem = pl.BlockSpec(memory_space=pltpu.VMEM)
    smem = pl.BlockSpec(memory_space=pltpu.SMEM)
    dma = pltpu.SemaphoreType.DMA
    scratch = (
        [pltpu.VMEM((2, half, tok, hd), BF) for _ in range(4)]
        + [pltpu.VMEM((2, half, 2 * tok, hd), BF) for _ in range(2)]
        + [
            pltpu.VMEM((2, 2, half, tok, hd), BF),
            pltpu.VMEM((2, 9, third, 2, tok, hd), BF),
            pltpu.VMEM((2, 6, third, 2, tok, hd), BF),
            pltpu.VMEM((9, 32, hd), F32),
        ]
        + [pltpu.VMEM((2, third, tok, hd), BF) for _ in range(6)]
        + [
            pltpu.VMEM((18, third, tok, hd), BF),
            pltpu.VMEM((18 * third, 2, 2 * tok, hd), BF),
            pltpu.VMEM((heads, 2, 2 * tok, hd), F32),
            pltpu.VMEM((heads, tok, hd), F32),
            pltpu.VMEM((2, 2, half, tok, hd), BF),
            pltpu.VMEM((2, 2, half, tok, hd), BF),
            pltpu.VMEM((2, 2, half, tok, hd), BF),
            pltpu.VMEM((2, 2, half, tok, hd), BF),
            pltpu.SMEM((18 * third,), jnp.int32),
            pltpu.SMEM((18 * half,), jnp.int32),
            pltpu.SMEM((18 * half,), jnp.int32),
            pltpu.SMEM((heads * 4,), jnp.int32),
        ]
    )
    for sem in ((2, 2), (2,), (2,), (2, 6), (6,), (2, 6), (2, 2), (2,)):
        scratch += [dma(sem), dma(sem)]
    dq, dk, dv = pl.pallas_call(
        functools.partial(kernel, n_sh, n_sw, half, hd),
        out_shape=[jax.ShapeDtypeStruct((tok, cols), BF)] * 3,
        in_specs=[vmem] * 6 + [smem],
        out_specs=[vmem] * 3,
        scratch_shapes=scratch,
        compiler_params=pltpu.CompilerParams(
            collective_id=0, has_side_effects=True, vmem_limit_bytes=40 * 2**20
        ),
    )(flat(queries), flat(keys), flat(values), flat(attn_grad), flat(attn_out), flat(log_sum), window_dirs)
    return tuple(array.reshape(shape) for array in (dq, dk, dv))


def solution(mesh):
    spec = P("tp", "sh", "sw", None)
    return jax.shard_map(
        functools.partial(local, mesh.shape["sh"], mesh.shape["sw"]),
        mesh=mesh,
        in_specs=(spec,) * 6 + (P(),),
        out_specs=(spec,) * 3,
        check_vma=False,
    )
```

time: 252 us -> 46.3 us (0.18)
  the two profiles are of different devices: /device:TPU:4 before, /device:TPU:0 now
where the time goes in v1:
time: 46.3 us; the launch traced here: 45.9 us
  Pallas kernels  37.1 us (80%)
  local copies, waits for them, and re-layouts  8.19 us (18%)
  between operations  0.65 us (1%)
    pallas_call x1, Pallas kernels, local(): pl.pallas_call(functools.partial(kernel, n_sh, n_sw, half, hd), out_shape...  37.1 us
    unnamed x18, local copies, waits for them, and re-layouts  8.19 us

profile of v1, /device:TPU:0, one launch (start us, length us, event | category | flops | bytes accessed | tf_op | source)
XLA Modules:
  0.0 45.9 jit_solution(213178185740091284)
XLA Ops:
  0.6 0.0 copy-start.6
  0.6 0.7 %copy-done.6 = s32[12,4]{0,1:T(4,128)S(1)} copy-done((s32[12,4]{0,1:T(4,128)S(1)}, s32[12,4]{0,1:T(4,128)}, u32[]{:S(2)}) %copy-start.6) | copy-done | bytes 216
  1.3 0.1 copy.10.wd_ref
  1.4 0.0 copy-start
  1.4 0.9 %copy-done = bf16[1,8,8,1536]{3,2,1,0:T(8,128)(2,1)S(1)} copy-done((bf16[1,8,8,1536]{3,2,1,0:T(8,128)(2,1)S(1)}, bf16[1,8,8,1536]{3,2,1,0:T(8,128)(2,1)}, u32[]{:S(2)}) %copy-start) | copy-done | bytes 196632
  2.3 0.0 copy-start.1
  2.3 0.9 %copy-done.1 = bf16[1,8,8,1536]{3,2,1,0:T(8,128)(2,1)S(1)} copy-done((bf16[1,8,8,1536]{3,2,1,0:T(8,128)(2,1)S(1)}, bf16[1,8,8,1536]{3,2,1,0:T(8,128)(2,1)}, u32[]{:S(2)}) %copy-start.1) | copy-done | bytes 196632
  3.3 0.0 copy-start.2
  3.3 0.9 %copy-done.2 = bf16[1,8,8,1536]{3,2,1,0:T(8,128)(2,1)S(1)} copy-done((bf16[1,8,8,1536]{3,2,1,0:T(8,128)(2,1)S(1)}, bf16[1,8,8,1536]{3,2,1,0:T(8,128)(2,1)}, u32[]{:S(2)}) %copy-start.2) | copy-done | bytes 196632
  4.2 0.0 copy-start.3
  4.2 0.9 %copy-done.3 = bf16[1,8,8,1536]{3,2,1,0:T(8,128)(2,1)S(1)} copy-done((bf16[1,8,8,1536]{3,2,1,0:T(8,128)(2,1)S(1)}, bf16[1,8,8,1536]{3,2,1,0:T(8,128)(2,1)}, u32[]{:S(2)}) %copy-start.3) | copy-done | bytes 196632
  5.1 0.0 copy-start.4
  5.1 0.9 %copy-done.4 = bf16[1,8,8,1536]{3,2,1,0:T(8,128)(2,1)S(1)} copy-done((bf16[1,8,8,1536]{3,2,1,0:T(8,128)(2,1)S(1)}, bf16[1,8,8,1536]{3,2,1,0:T(8,128)(2,1)}, u32[]{:S(2)}) %copy-start.4) | copy-done | bytes 196632
  6.0 0.0 copy-start.5
  6.0 0.8 %copy-done.5 = f32[1,8,8,12]{3,2,1,0:T(8,128)S(1)} copy-done((f32[1,8,8,12]{3,2,1,0:T(8,128)S(1)}, f32[1,8,8,12]{3,2,1,0:T(8,128)}, u32[]{:S(2)}) %copy-start.5) | copy-done | bytes 3096
  6.8 37.1 %shard_map.94 = (bf16[64,1536]{1,0:T(8,128)(2,1)S(1)}, bf16[64,1536]{1,0:T(8,128)(2,1)S(1)}, bf16[64,1536]{1,0:T(8,128)(2,1)S(1)}) custom-call(bf16[64,1536]{1,0:T(8,128)(2,1)S(1)} %bitcast.12, bf16[64,1536]{1,0:T(8,128)(2,1)S(1)} %bitcast.13, bf16[64,1536]{1,0:T(8,128)(2,1)S(1)} %bitcast.14, bf16[64,1536]{1,0:T(8,128)(2,1)S(1)} %bitcast.15, ...), custom_call_target="tpu_custom_call" | custom-call | tf_op jit(solution)/shard_map/pallas_call | solution.py:431
  43.9 0.7 %copy.14 = bf16[1,8,8,1536]{3,2,1,0:T(8,128)(2,1)} copy(bf16[1,8,8,1536]{3,2,1,0:T(8,128)(2,1)S(1)} %bitcast.11) | data formatting | bytes 393216
  44.6 0.7 %copy.15 = bf16[1,8,8,1536]{3,2,1,0:T(8,128)(2,1)} copy(bf16[1,8,8,1536]{3,2,1,0:T(8,128)(2,1)S(1)} %bitcast.10) | data formatting | bytes 393216
  45.3 0.7 %copy.16 = bf16[1,8,8,1536]{3,2,1,0:T(8,128)(2,1)} copy(bf16[1,8,8,1536]{3,2,1,0:T(8,128)(2,1)S(1)} %bitcast.9) | data formatting | bytes 393216
Async XLA Ops:
  0.6 0.7 %copy-start.6 = (s32[12,4]{0,1:T(4,128)S(1)}, s32[12,4]{0,1:T(4,128)}, u32[]{:S(2)}) copy-start(s32[12,4]{0,1:T(4,128)} %param.13) | copy-start | bytes 580
  1.4 0.9 %copy-start = (bf16[1,8,8,1536]{3,2,1,0:T(8,128)(2,1)S(1)}, bf16[1,8,8,1536]{3,2,1,0:T(8,128)(2,1)}, u32[]{:S(2)}) copy-start(bf16[1,8,8,1536]{3,2,1,0:T(8,128)(2,1)} %param.7) | copy-start | bytes 589828
  2.3 0.9 %copy-start.1 = (bf16[1,8,8,1536]{3,2,1,0:T(8,128)(2,1)S(1)}, bf16[1,8,8,1536]{3,2,1,0:T(8,128)(2,1)}, u32[]{:S(2)}) copy-start(bf16[1,8,8,1536]{3,2,1,0:T(8,128)(2,1)} %param.8) | copy-start | bytes 589828
  3.3 0.9 %copy-start.2 = (bf16[1,8,8,1536]{3,2,1,0:T(8,128)(2,1)S(1)}, bf16[1,8,8,1536]{3,2,1,0:T(8,128)(2,1)}, u32[]{:S(2)}) copy-start(bf16[1,8,8,1536]{3,2,1,0:T(8,128)(2,1)} %param.9) | copy-start | bytes 589828
  4.2 0.9 %copy-start.3 = (bf16[1,8,8,1536]{3,2,1,0:T(8,128)(2,1)S(1)}, bf16[1,8,8,1536]{3,2,1,0:T(8,128)(2,1)}, u32[]{:S(2)}) copy-start(bf16[1,8,8,1536]{3,2,1,0:T(8,128)(2,1)} %param.11) | copy-start | bytes 589828
  5.1 0.9 %copy-start.4 = (bf16[1,8,8,1536]{3,2,1,0:T(8,128)(2,1)S(1)}, bf16[1,8,8,1536]{3,2,1,0:T(8,128)(2,1)}, u32[]{:S(2)}) copy-start(bf16[1,8,8,1536]{3,2,1,0:T(8,128)(2,1)} %param.10) | copy-start | bytes 589828
  6.0 0.8 %copy-start.5 = (f32[1,8,8,12]{3,2,1,0:T(8,128)S(1)}, f32[1,8,8,12]{3,2,1,0:T(8,128)}, u32[]{:S(2)}) copy-start(f32[1,8,8,12]{3,2,1,0:T(8,128)} %param.12) | copy-start | bytes 9220

commit v2 on v1

--- a/solution.py
+++ b/solution.py
@@ -16,9 +16,10 @@
 
 def kernel(
     n_sh, n_sw, half, hd,
-    q_ref, k_ref, v_ref, g_ref, o_ref, lse_ref, wd_ref,
+    q_in, k_in, v_in, g_in, o_in, lse_in, wd_in,
     dq_out, dk_out, dv_out,
     zb00, zb01, zb10, zb11, kv0, kv1, qg, pieces, packed, stats,
+    q_ref, k_ref, v_ref, g_ref, o_ref, lse_ref, wd_ref, in_sem,
     rs00, rs01, rs02, rs10, rs11, rs12, dqs, dkp, own_kv, own_q,
     zsend, zback, xsend, xback, head_of, rank_of, member_of, flat_of,
     zs, zr, zts, ztr, xs, xr, ws, wr, wts, wtr, rs, rr, rzs, rzr, rxs, rxr,
@@ -31,6 +32,12 @@
     rsw = ((rs00, rs01, rs02), (rs10, rs11, rs12))
     third = half // 2
     tok = q_ref.shape[0]
+    arguments = (
+        (q_in, q_ref), (g_in, g_ref), (k_in, k_ref), (v_in, v_ref), (wd_in, wd_ref), (o_in, o_ref), (lse_in, lse_ref),
+    )
+    loads = [pltpu.make_async_copy(src, dst, in_sem.at[i]) for i, (src, dst) in enumerate(arguments)]
+    for load in loads:
+        load.start()
     scale = hd ** -0.5
     row_ok = lambda step: (row + step >= 0) & (row + step < n_sh)
     col_ok = lambda step: (col + step >= 0) & (col + step < n_sw)
@@ -82,27 +89,34 @@
         @pl.when(col_ok(step))
         def _():
             pl.semaphore_signal(barrier, inc=1, device_id={"sw": col + step}, device_id_type=pl.DeviceIdType.MESH)
+    count = 1
+    for step in (-1, 1):
+        count = count + row_ok(step).astype(jnp.int32) + col_ok(step).astype(jnp.int32)
+    pl.semaphore_wait(barrier, count)
+
+    loads[0].wait()
+    loads[1].wait()
     for run in (0, 1):
         for h in range(half):
             cols = slice((run * half + h) * hd, (run * half + h + 1) * hd)
             qg[run, 0, h] = q_ref[:, cols]
             qg[run, 1, h] = g_ref[:, cols]
+        for i in (0, 1):
+            @pl.when(row_ok(2 * i - 1))
+            def _():
+                copy_z(run, i).start()
+    loads[2].wait()
+    loads[3].wait()
+    for run in (0, 1):
+        for h in range(half):
+            cols = slice((run * half + h) * hd, (run * half + h + 1) * hd)
             kv[run][0, h, :tok] = k_ref[:, cols]
             kv[run][1, h, :tok] = v_ref[:, cols]
-    count = 1
-    for step in (-1, 1):
-        count = count + row_ok(step).astype(jnp.int32) + col_ok(step).astype(jnp.int32)
-    pl.semaphore_wait(barrier, count)
-
-    for run in (0, 1):
-        for i in (0, 1):
-            @pl.when(row_ok(2 * i - 1))
-            def _():
-                copy_z(run, i).start()
         copy_x(run).start()
 
-    for run in (0, 1):
-        dirs = [[wd_ref[run * half + h, j] for j in range(4)] for h in range(half)]
+    loads[4].wait()
+    for run in (0, 1):
+        dirs = [[wd_ref[j, run * half + h] for j in range(4)] for h in range(half)]
         flat = [[jnp.int32(0) for j in range(4)] for h in range(half)]
         for d in range(8):
             e = E_OF[d]
@@ -144,6 +158,8 @@
                 pack(run, c, 0)
                 copy_w(run, c, 0).start()
 
+    loads[5].wait()
+    loads[6].wait()
     lane = lax.broadcasted_iota(jnp.int32, (tok, hd), 1)
     table = jnp.zeros((tok, hd), F32)
     for run in (0, 1):
@@ -336,26 +352,26 @@
 
         lax.fori_loop(0, half, body, 0)
 
+    relay(0)
     copy_x(0).wait_recv()
     own(0)
-    relay(0)
-    from_rows(0)
     from_side(0, 0, 0)
     from_side(0, 1, 0)
+    relay(1)
+    from_rows(0)
+    for i in (1, 2):
+        for c in (0, 1):
+            from_side(0, c, i)
+    to_partner(0)
     copy_x(1).wait_recv()
-    relay(1)
-    for c in (0, 1):
-        for i in (1, 2):
-            from_side(0, c, i)
     from_rows(1)
-    to_partner(0)
     turn(0)
-    own(1)
+    for i in (1, 2):
+        for c in (0, 1):
+            from_side(1, c, i)
     from_side(1, 0, 0)
     from_side(1, 1, 0)
-    for c in (0, 1):
-        for i in (1, 2):
-            from_side(1, c, i)
+    own(1)
     to_partner(1)
     turn(1)
     finish_kv(0)
@@ -387,6 +403,18 @@
                 @pl.when(row_ok(-row_step[i]) & col_ok(-col_step[c]))
                 def _():
                     copy_back(run, c, i).wait_send()
+
+
+def hand_out(a_in, b_in, c_in, a_out, b_out, c_out, held, in_sem, out_sem):
+    ins = [pltpu.make_async_copy(src, held.at[i], in_sem.at[i]) for i, src in enumerate((a_in, b_in, c_in))]
+    outs = [pltpu.make_async_copy(held.at[i], dst, out_sem.at[i]) for i, dst in enumerate((a_out, b_out, c_out))]
+    for copy in ins:
+        copy.start()
+    for first, second in zip(ins, outs):
+        first.wait()
+        second.start()
+    for copy in outs:
+        copy.wait()
 
 
 def local(n_sh, n_sw, queries, keys, values, attn_out, attn_grad, log_sum, window_dirs):
@@ -399,7 +427,7 @@
     hd = cols // heads
     flat = lambda array: array.reshape(tok, array.shape[3])
     vmem = pl.BlockSpec(memory_space=pltpu.VMEM)
-    smem = pl.BlockSpec(memory_space=pltpu.SMEM)
+    hbm = pl.BlockSpec(memory_space=pltpu.HBM)
     dma = pltpu.SemaphoreType.DMA
     scratch = (
         [pltpu.VMEM((2, half, tok, hd), BF) for _ in range(4)]
@@ -410,6 +438,8 @@
             pltpu.VMEM((2, 6, third, 2, tok, hd), BF),
             pltpu.VMEM((9, 32, hd), F32),
         ]
+        + [pltpu.VMEM((tok, cols), BF) for _ in range(5)]
+        + [pltpu.VMEM((tok, heads), F32), pltpu.SMEM((4, heads), jnp.int32), dma((7,))]
         + [pltpu.VMEM((2, third, tok, hd), BF) for _ in range(6)]
         + [
             pltpu.VMEM((18, third, tok, hd), BF),
@@ -431,13 +461,21 @@
     dq, dk, dv = pl.pallas_call(
         functools.partial(kernel, n_sh, n_sw, half, hd),
         out_shape=[jax.ShapeDtypeStruct((tok, cols), BF)] * 3,
-        in_specs=[vmem] * 6 + [smem],
+        in_specs=[hbm] * 7,
         out_specs=[vmem] * 3,
         scratch_shapes=scratch,
         compiler_params=pltpu.CompilerParams(
-            collective_id=0, has_side_effects=True, vmem_limit_bytes=40 * 2**20
+            collective_id=0, has_side_effects=True, vmem_limit_bytes=64 * 2**20
         ),
-    )(flat(queries), flat(keys), flat(values), flat(attn_grad), flat(attn_out), flat(log_sum), window_dirs)
+    )(flat(queries), flat(keys), flat(values), flat(attn_grad), flat(attn_out), flat(log_sum), window_dirs.T)
+    dq, dk, dv = pl.pallas_call(
+        hand_out,
+        out_shape=[jax.ShapeDtypeStruct((tok, cols), BF)] * 3,
+        in_specs=[hbm] * 3,
+        out_specs=[hbm] * 3,
+        scratch_shapes=[pltpu.VMEM((3, tok, cols), BF), dma((3,)), dma((3,))],
+        compiler_params=pltpu.CompilerParams(vmem_limit_bytes=64 * 2**20),
+    )(dq, dk, dv)
     return tuple(array.reshape(shape) for array in (dq, dk, dv))
 
 

time: 46.3 us -> 38.8 us (0.84)
  the two profiles are of different devices: /device:TPU:0 before, /device:TPU:9 now
where the time goes in v2:
time: 38.8 us; the launch traced here: 38.6 us
  Pallas kernels  38 us (98%)
  between operations  0.64 us (2%)
    pallas_call x1, Pallas kernels, local(): pl.pallas_call(functools.partial(kernel, n_sh, n_sw, half, hd), out_shape...  36.2 us
    pallas_call x1, Pallas kernels, local(): pl.pallas_call(hand_out, out_shape=[jax.ShapeDtypeStruct((tok, cols), BF)...  1.84 us

profile of v2, /device:TPU:9, one launch (start us, length us, event | category | flops | bytes accessed | tf_op | source)
XLA Modules:
  0.0 38.6 jit_solution(10789330469647260417)
XLA Ops:
  0.6 36.2 %shard_map.94 = (bf16[64,1536]{1,0:T(8,128)(2,1)}, bf16[64,1536]{1,0:T(8,128)(2,1)}, bf16[64,1536]{1,0:T(8,128)(2,1)}) custom-call(bf16[64,1536]{1,0:T(8,128)(2,1)} %bitcast.10, bf16[64,1536]{1,0:T(8,128)(2,1)} %bitcast.11, bf16[64,1536]{1,0:T(8,128)(2,1)} %bitcast.12, bf16[64,1536]{1,0:T(8,128)(2,1)} %bitcast.13, bf16[64,1536]{1,0:T(8,128)(2,1)} %bitcast.14, ...), custom_call_target="tpu_custom_call" | custom-call | tf_op jit(solution)/shard_map/pallas_call | solution.py:461
  36.8 1.8 %shard_map.95 = (bf16[64,1536]{1,0:T(8,128)(2,1)}, bf16[64,1536]{1,0:T(8,128)(2,1)}, bf16[64,1536]{1,0:T(8,128)(2,1)}) custom-call(bf16[64,1536]{1,0:T(8,128)(2,1)} %get-tuple-element.9.a_in, bf16[64,1536]{1,0:T(8,128)(2,1)} %get-tuple-element.10.b_in, bf16[64,1536]{1,0:T(8,128)(2,1)} %get-tuple-element.11.c_in), custom_call_target="tpu_custom_call" | custom-call | tf_op jit(solution)/shard_map/pallas_call | solution.py:471
